TPU v7x, 512 devices: a whole 4x8x8 slice. The times are simulated.
512 devices in a mesh: ctx: 64 (over y_lo, z, core), tp: 8 (over y_hi, x).
Axes of the slice: x: 4, y: 8 (y_hi: 2, y_lo: 4; y = y_hi * 4 + y_lo), z: 8, core: 2. Of those that a mesh axis runs over, the one named last changes fastest.
Arguments:
- vision_rows: bfloat16 [64, 160, 3584], P('ctx', None, 'tp'), may hold values from -10 to 10
- audio_rows: bfloat16 [64, 64, 1280], P('ctx'), may hold values from -6 to 6
- vision_count: int32 [64], replicated, may hold values from 1 to 160, 6144 in all
- audio_count: int32 [64], replicated, may hold values from 1 to 64, 2048 in all
- position_ids: int32 [3, 64, 224], P(None, 'ctx'), may hold values from 0 to 14335
- audio_proj: bfloat16 [1280, 3584], P(None, 'tp'), may hold values from -0.15625 to 0.15625
- norm_gain: float32 [3584], replicated, may hold values from 0.1 to 1.9
- q_weight: bfloat16 [3584, 2048], P(None, 'tp'), may hold values from -1 to 1
- key_value_weight: bfloat16 [3584, 512], P('tp'), may hold values from -1 to 1
Outputs:
- attended: bfloat16 [64, 224, 2048], P('ctx', None, 'tp')
Inputs may be any that keep to these rules, and one draw needn't show every extreme that they name: `vision_count`: sum to 6144, the largest is exactly 160. `audio_count`: sum to 2048, the largest is exactly 64.
All inputs are finite; a program needn't handle non-finite values.
Results may differ from a plain program's by a relative error of at most 0.017.
Values may be sent and summed in bfloat16 or wider, within the bound.
A program may use at most 64 MiB of HBM per device.

v0:
```python
import math

import jax
import jax.numpy as jnp
import numpy as np
from jax import lax
from jax.sharding import PartitionSpec as P

HEAD_WIDTH = 128
QUERY_HEADS = 16
KEY_VALUE_HEADS = 2


def section_index(half_size):
    first = half_size // 4
    second = (half_size - first) // 2
    return np.array([0] * first + [1] * second + [2] * (half_size - first - second), dtype=np.int32)


def rope_tables(position_ids, head_size):
    half_size = head_size // 2
    chosen = position_ids[section_index(half_size)].astype(jnp.float32)
    chosen = jnp.moveaxis(chosen, 0, -1)
    inverse = jnp.exp(
        -math.log(1000000.0) * 2.0 * jnp.arange(half_size, dtype=jnp.float32) / head_size
    )
    angle_table = chosen * inverse
    return (jnp.cos(angle_table), jnp.sin(angle_table))


def rotate(values_in, cosine_table, sine_table):
    half_size = values_in.shape[-1] // 2
    first = values_in[..., :half_size]
    second = values_in[..., half_size:]
    cosine_b = cosine_table[..., None, :]
    sine_b = sine_table[..., None, :]
    return jnp.concatenate(
        [first * cosine_b - second * sine_b, second * cosine_b + first * sine_b], axis=-1
    )


def lookup(table, stretch_ids, wanted):
    return jnp.sum(jnp.where(stretch_ids == wanted, table, 0))


def attend(
    head_queries,
    key_part,
    value_part,
    row_offset,
    part_rows,
    query_pos,
    starts,
    totals,
    stretch_ids,
):
    head_count = head_queries.shape[1]
    slot_count = head_queries.shape[0]
    scale = HEAD_WIDTH ** (-0.5)
    local_rows = jnp.arange(part_rows, dtype=jnp.int32)
    initial = (
        jnp.full((head_count, slot_count), -1e30, jnp.float32),
        jnp.zeros((head_count, slot_count), jnp.float32),
        jnp.zeros((head_count, slot_count, HEAD_WIDTH), jnp.float32),
    )
    key_piece = lax.all_gather(key_part, "ctx", axis=0, tiled=True)
    value_piece = lax.all_gather(value_part, "ctx", axis=0, tiled=True)
    block_count = key_piece.shape[0] // part_rows

    def update(block_id, carried):
        run_max, run_sum, run_acc = carried
        key_block = lax.dynamic_slice_in_dim(key_piece, block_id * part_rows, part_rows, 0)
        value_block = lax.dynamic_slice_in_dim(value_piece, block_id * part_rows, part_rows, 0)
        stretch_start = lookup(starts, stretch_ids, block_id)
        stretch_total = lookup(totals, stretch_ids, block_id)
        key_pos = stretch_start + row_offset + local_rows
        key_live = row_offset + local_rows < stretch_total
        scores = (
            jnp.einsum("qhd,kd->hqk", head_queries, key_block, preferred_element_type=jnp.float32)
            * scale
        )
        counted = (key_pos[None, :] <= query_pos[:, None]) & key_live[None, :]
        scores = jnp.where(counted[None], scores, -1e30)
        new_max = jnp.maximum(run_max, jnp.max(scores, axis=-1))
        weights = jnp.where(counted[None], jnp.exp(scores - new_max[..., None]), 0.0)
        factor = jnp.exp(run_max - new_max)
        run_sum = run_sum * factor + jnp.sum(weights, axis=-1)
        run_acc = run_acc * factor[..., None] + jnp.einsum(
            "hqk,kd->hqd",
            weights.astype(jnp.bfloat16),
            value_block,
            preferred_element_type=jnp.float32,
        )
        return (new_max, run_sum, run_acc)

    def block_step(block_id, carried):
        return update(block_id, carried)

    return lax.fori_loop(0, block_count, block_step, initial)


def per_device(
    vision_rows,
    audio_rows,
    vision_count,
    audio_count,
    position_ids,
    audio_proj,
    norm_gain,
    q_weight,
    key_value_weight,
):
    vision_slots = vision_rows.shape[1]
    stretch_slots = vision_slots + audio_rows.shape[1]
    heads_here = q_weight.shape[1] // HEAD_WIDTH
    ctx_index = lax.axis_index("ctx")
    tp_index = lax.axis_index("tp")
    totals = vision_count + audio_count
    starts = jnp.cumsum(totals) - totals
    stretch_ids = jnp.arange(totals.shape[0], dtype=jnp.int32)
    own_vision = lookup(vision_count, stretch_ids, ctx_index)
    own_total = lookup(totals, stretch_ids, ctx_index)
    own_start = lookup(starts, stretch_ids, ctx_index)
    audio_part = jnp.dot(audio_rows[0], audio_proj, preferred_element_type=jnp.float32).astype(
        jnp.bfloat16
    )
    stacked = jnp.concatenate([vision_rows[0], audio_part], axis=0)
    slot_rows = jnp.arange(stretch_slots, dtype=jnp.int32)
    source_index = jnp.where(
        slot_rows < own_vision, slot_rows, vision_slots + slot_rows - own_vision
    )
    source_index = jnp.clip(source_index, 0, stretch_slots - 1)
    slot_live = slot_rows < own_total
    slots = jnp.where(slot_live[:, None], stacked[source_index], jnp.zeros_like(stacked))
    features = lax.all_gather(slots, "tp", axis=1, tiled=True)
    feature_f32 = features.astype(jnp.float32)
    mean_square = jnp.mean(feature_f32 * feature_f32, axis=-1, keepdims=True)
    normed = (feature_f32 * lax.rsqrt(mean_square + 1e-06) * norm_gain).astype(jnp.bfloat16)
    cosine_table, sine_table = rope_tables(position_ids[:, 0], HEAD_WIDTH)
    queries = jnp.dot(normed, q_weight, preferred_element_type=jnp.float32).reshape(
        stretch_slots, heads_here, HEAD_WIDTH
    )
    queries = rotate(queries, cosine_table, sine_table).astype(jnp.bfloat16)
    key_value_full = jnp.dot(
        normed,
        lax.all_gather(key_value_weight, "tp", axis=0, tiled=True),
        preferred_element_type=jnp.float32,
    )
    head_group = QUERY_HEADS // KEY_VALUE_HEADS
    key_value_head = tp_index * heads_here // head_group
    key_raw = lax.dynamic_slice_in_dim(key_value_full, key_value_head * HEAD_WIDTH, HEAD_WIDTH, 1)
    value_unscaled = lax.dynamic_slice_in_dim(
        key_value_full, (KEY_VALUE_HEADS + key_value_head) * HEAD_WIDTH, HEAD_WIDTH, 1
    )
    key_rows = rotate(key_raw[:, None, :], cosine_table, sine_table)[:, 0].astype(jnp.bfloat16)
    value_rows = value_unscaled.astype(jnp.bfloat16)
    query_pos = own_start + slot_rows
    run_max, run_sum, run_acc = attend(
        queries, key_rows, value_rows, 0, stretch_slots, query_pos, starts, totals, stretch_ids
    )
    denom = jnp.where(slot_live[None, :], run_sum, 1.0)
    result = jnp.where(slot_live[None, :, None], run_acc / denom[..., None], 0.0)
    result = jnp.transpose(result, (1, 0, 2)).reshape(stretch_slots, heads_here * HEAD_WIDTH)
    return result.astype(jnp.bfloat16)[None]


def solution(mesh):
    placed = (
        P("ctx", None, "tp"),
        P("ctx", None, None),
        P(),
        P(),
        P(None, "ctx", None),
        P(None, "tp"),
        P(),
        P(None, "tp"),
        P("tp", None),
    )
    return jax.shard_map(
        per_device, mesh=mesh, in_specs=placed, out_specs=P("ctx", None, "tp"), check_vma=False
    )
```

profile of v0, /device:TPU:56, one launch (start us, length us, event | category | flops | bytes accessed | tf_op | source)
XLA Modules:
  0.0 782.4 jit_solution(4152805477098534248)
XLA Ops:
  6.6 1.5 select_reduce_fusion.2
  9.5 1.8 convolution_convert_fusion
  15.8 74.8 %all-gather.6.cloned.1.call-done = bf16[224,3584]{0,1:T(8,128)(2,1)} async-done(((bf16[224,448]{0,1:T(8,128)(2,1)}), bf16[224,3584]{0,1:T(8,128)(2,1)}) %all-gather.6.cloned.1.call-update) | async-done | bytes 1605648 | tf_op jit(solution)/shard_map/all_gather | solution.py:135
  90.6 2.0 fusion.25
  92.7 98.4 %all-gather.8.cloned.1.call-done = bf16[3584,512]{1,0:T(8,128)(2,1)} async-done(((bf16[448,512]{1,0:T(8,128)(2,1)}), bf16[3584,512]{1,0:T(8,128)(2,1)}) %all-gather.8.cloned.1.call-update) | async-done | bytes 3670032 | tf_op jit(solution)/shard_map/all_gather | solution.py:146
  191.1 4.7 fusion.30
  199.3 2.7 fusion.28
  202.7 119.2 %all-gather.12.cloned.1.call-done = bf16[14336,1,128]{2,0,1:T(8,128)(2,1)} async-done(((bf16[224,1,128]{2,0,1:T(8,128)(2,1)}), bf16[14336,1,128]{2,0,1:T(8,128)(2,1)}) %all-gather.12.cloned.1.call-update) | async-done | bytes 3670032 | tf_op jit(solution)/shard_map/all_gather | solution.py:66
  321.9 120.0 %all-gather.10.cloned.1.call-done = bf16[14336,128]{1,0:T(8,128)(2,1)} async-done(((bf16[224,128]{1,0:T(8,128)(2,1)}), bf16[14336,128]{1,0:T(8,128)(2,1)}) %all-gather.10.cloned.1.call-update) | async-done | bytes 3670032 | tf_op jit(solution)/shard_map/all_gather | solution.py:67
  441.8 333.1 %while.19 = (s32[]{:T(128)}, f32[2,224]{1,0:T(2,128)S(1)}, f32[2,224]{1,0:T(2,128)S(1)}, f32[2,224,128]{2,1,0:T(8,128)S(1)}, s32[64]{0:T(128)S(1)}, /*index=5*/s...) while((s32[]{:T(128)}, f32[2,224]{1,0:T(2,128)S(1)}, ...), condition=%wide.region_10.11_spmd.clone.clone, body=%wide.region_5.10_spmd.clone.clone.sunk | while | flops 52559012 | bytes 2126503 | solution.py:99
  445.9 1.1 convolution_add_fusion.2
  451.1 1.1 convolution_add_fusion.2
  456.3 1.1 convolution_add_fusion.2
  461.5 1.1 convolution_add_fusion.2
  466.7 1.1 convolution_add_fusion.2
  471.9 1.1 convolution_add_fusion.2
  477.1 1.1 convolution_add_fusion.2
  482.3 1.1 convolution_add_fusion.2
  529.1 1.1 convolution_add_fusion.2
  539.6 1.1 convolution_add_fusion.2
  628.0 1.1 convolution_add_fusion.2
  638.4 1.1 convolution_add_fusion.2
  726.9 1.1 convolution_add_fusion.2
  737.3 1.1 convolution_add_fusion.2
  (744 shorter events, 322.7 us)
Async XLA Ops:
  6.5 192.8 %copy-start = (bf16[3584,256]{1,0:T(8,128)(2,1)S(1)}, bf16[3584,256]{1,0:T(8,128)(2,1)}, u32[]{:S(2)}) copy-start(bf16[3584,256]{1,0:T(8,128)(2,1)} %param.20) | copy-start | bytes 5505028
  6.5 8.6 %copy-start.2 = (s32[64]{0:T(128)S(1)}, s32[64]{0:T(128)}, u32[]{:S(2)}) copy-start(s32[64]{0:T(128)} %constant.125) | copy-start | bytes 772
  6.5 8.6 %copy-start.1 = (s32[3,1,224]{2,1,0:T(1,128)S(1)}, s32[3,1,224]{2,1,0:T(1,128)}, u32[]{:S(2)}) copy-start(s32[3,1,224]{2,1,0:T(1,128)} %param.17) | copy-start | bytes 8068
  6.5 84.1 %all-gather.6.cloned.1.call-start = ((), (), s32[]{:S(2)}) async-start(), calls=%async_computation | async-start | bytes 2064384 | tf_op jit(solution)/shard_map/all_gather | solution.py:135
  9.5 181.6 %copy-start.3 = (f32[3584]{0:T(1024)S(1)}, f32[3584]{0:T(1024)}, u32[]{:S(2)}) copy-start(f32[3584]{0:T(1024)} %param.19) | copy-start | bytes 43012
  14.3 176.8 %all-gather.8.cloned.1.call-start = ((), (), s32[]{:S(2)}) async-start(), calls=%async_computation.1 | async-start | bytes 4128768 | tf_op jit(solution)/shard_map/all_gather | solution.py:146
  15.1 306.8 %all-gather.12.cloned.1.call-start = ((), (), s32[]{:S(2)}) async-start(), calls=%async_computation.3 | async-start | bytes 3727360 | tf_op jit(solution)/shard_map/all_gather | solution.py:66
  197.1 244.7 %all-gather.10.cloned.1.call-start = ((), (), s32[]{:S(2)}) async-start(), calls=%async_computation.2 | async-start | bytes 3727360 | tf_op jit(solution)/shard_map/all_gather | solution.py:67
Sparse Core Ops, SparseCore 0:
  14.4 76.1 all-gather.5
  93.8 97.1 all-gather.7
  197.2 124.5 all-gather.11
  323.9 117.9 all-gather.9
where the time goes:
time: 791 us; the launch traced here: 782 us
  waiting for transfers between devices  413 us (52%)
  other arithmetic  193 us (24%)
  matrix products  152 us (19%)
  between operations  13.4 us (2%)
    all_gather x1, waiting for transfers between devices, attend(): value_piece = lax.all_gather(value_part, 'ctx', axis=0, tiled=True)  120 us
    all_gather x1, waiting for transfers between devices, attend(): key_piece = lax.all_gather(key_part, 'ctx', axis=0, tiled=True)  119 us
    all_gather x1, waiting for transfers between devices, per_device(): lax.all_gather(key_value_weight, 'tp', axis=0, tiled=True)  98.4 us
    all_gather x1, waiting for transfers between devices, per_device(): features = lax.all_gather(slots, 'tp', axis=1, tiled=True)  74.8 us
    dot_general x64, matrix products, update(): jnp.einsum('hqk,kd->hqd', weights.astype(jnp.bfloat16), value_block, pref...  72.8 us
    dot_general x64, matrix products, update(): jnp.einsum('qhd,kd->hqk', head_queries, key_block, preferred_element_type...  69.6 us
    reduce_sum x66, other arithmetic, lookup(): return jnp.sum(jnp.where(stretch_ids == wanted, table, 0))  48 us
    lt x64, other arithmetic, update(): key_live = row_offset + local_rows < stretch_total  44.3 us
  transfers between devices with their start and end apart: 4, of which 4 were waited for; matrix products, arithmetic and copies ran while one was open for 1% of the time, Pallas kernels for 0%

commit v1 on v0

v1 whole, which is shorter than its diff:
```python
import functools
import math

import jax
import jax.numpy as jnp
import numpy as np
from jax import lax
from jax.experimental import pallas as pl
from jax.experimental.pallas import tpu as pltpu
from jax.sharding import PartitionSpec as P

HW = 128
MESH = pl.DeviceIdType.MESH
F32 = jnp.float32
BF16 = jnp.bfloat16

NY, NZ, NC, NX = 4, 8, 2, 4
VC, AC, T = 160, 64, 224
DS, D = 448, 3584
CH = 64
LIVE_CH = T // NX
HALF = T // 2
KB = 512
NEG = -1e30
QSCALE = HW**-0.5 * math.log2(math.e)


def iota(shape, dim):
    return lax.broadcasted_iota(jnp.int32, shape, dim)


def place():
    ctx, tp = lax.axis_index("ctx"), lax.axis_index("tp")
    return dict(yl=ctx // (NZ * NC), z=(ctx // NC) % NZ, core=ctx % NC, h=tp // NX, x=tp % NX, ctx=ctx, tp=tp)


def device(at, yl=None, z=None, core=None, h=None, x=None):
    yl = at["yl"] if yl is None else yl
    z = at["z"] if z is None else z
    core = at["core"] if core is None else core
    h = at["h"] if h is None else h
    x = at["x"] if x is None else x
    return ((yl * NZ + z) * NC + core, h * NX + x)


def along_y(at, by):
    y = (at["h"] * NY + at["yl"] + by) % (2 * NY)
    return device(at, h=y // NY, yl=y % NY)


def swap_halves(a):
    return jnp.concatenate([a[:, HW // 2 :], a[:, : HW // 2]], axis=1)


def rope(a, cos, sin):
    return a * cos + swap_halves(a) * sin


def tables(pos_ref, inv_ref, pick):
    rows = pick.shape[0]
    ids = [
        jnp.sum(jnp.where(pick, pos_ref[k].astype(F32), 0.0), axis=1, keepdims=True) for k in range(3)
    ]
    lane = iota((rows, HW), 1)
    freq = lane % (HW // 2)
    first = HW // 8
    second = (HW // 2 - first) // 2
    chosen = jnp.where(freq < first, ids[0], jnp.where(freq < first + second, ids[1], ids[2]))
    angle = chosen * inv_ref[...]
    sin = jnp.sin(angle)
    return jnp.cos(angle), jnp.where(lane < HW // 2, -sin, sin)


def gather_kernel(
    vcount, acount, pos_ref, inv_ref, gain_ref, vision_ref, audio_ref, proj_ref, kvw_ref, qw_hbm,
    q_out, kv_out,
    stacked, feat, via, part, rsbuf, qw, qw_sem, ssem, rsem,
):
    at = place()
    ctx, tp, x, h = at["ctx"], at["tp"], at["x"], at["h"]
    fetch = pltpu.make_async_copy(qw_hbm, qw, qw_sem)
    fetch.start()

    right = device(at, x=(x + 1) % NX)
    left = device(at, x=(x + 3) % NX)
    up = device(at, z=(at["z"] + 1) % NZ)
    down = device(at, z=(at["z"] + 7) % NZ)
    sibling = device(at, core=1 - at["core"])
    y_plus, y_minus = along_y(at, 2), along_y(at, 6)
    tp_peers = [(ctx, (tp + e) % 8) for e in range(1, 8)]
    y_peers = [device(at, yl=(at["yl"] + e) % NY) for e in range(1, NY)]
    greeted = [up, down, sibling, y_plus, y_minus] + tp_peers + y_peers
    barrier = pltpu.get_barrier_semaphore()
    for other in greeted:
        pl.semaphore_signal(barrier, inc=1, device_id=other, device_id_type=MESH)

    copies = []

    def remote(src, dst, to):
        i = len(copies)
        copy = pltpu.make_async_remote_copy(
            src_ref=src, dst_ref=dst, send_sem=ssem.at[i], recv_sem=rsem.at[i], device_id=to, device_id_type=MESH
        )
        copies.append(copy)
        copy.start()
        return copy

    vision_here = vcount[ctx]
    total = vision_here + acount[ctx]
    stacked[:VC] = vision_ref[0]
    stacked[VC:] = jnp.dot(audio_ref[0], proj_ref[...], preferred_element_type=F32).astype(BF16)

    def picked(slot, valid):
        source = jnp.where(slot < vision_here, slot, VC + slot - vision_here)
        hit = (iota((slot.shape[0], T), 1) == source) & (slot < total) & valid
        onehot = jnp.where(hit, 1.0, 0.0).astype(BF16)
        return jnp.dot(onehot, stacked[...], preferred_element_type=F32)

    slot = iota((T, 1), 0)
    feat[0, 0] = picked(slot, slot >= 0).astype(BF16)
    pl.semaphore_wait(barrier, len(greeted))

    top, low = pl.ds(0, HALF), pl.ds(HALF, HALF)
    via_plus = remote(feat.at[0, 0, top], via.at[0], y_plus)
    via_minus = remote(feat.at[0, 0, low], via.at[1], y_minus)
    from_left = [remote(feat.at[0, 0], feat.at[0, 3], right), None]
    from_right = [remote(feat.at[0, 0], feat.at[0, 1], left), None]

    row = iota((NX * CH, 1), 0)
    chunk_row = row % CH
    chunked = picked(chunk_row * NX + row // CH, chunk_row < LIVE_CH)
    squares = jnp.sum(chunked * chunked, axis=1, keepdims=True)
    gained = (chunked * gain_ref[pl.ds(tp, 1)]).astype(BF16)
    term = jnp.dot(gained, kvw_ref[...], preferred_element_type=F32)
    crow, clane = iota((CH, 2 * HW), 0), iota((CH, 2 * HW), 1)
    for g in range(2):
        for j in range(NX):
            rows = slice(j * CH, (j + 1) * CH)
            keys = term[rows, g * HW : (g + 1) * HW]
            values = term[rows, (2 + g) * HW : (3 + g) * HW]
            line = jnp.sum(jnp.where(crow == clane, squares[rows], 0.0), axis=0, keepdims=True)
            high = line.astype(BF16).astype(F32)
            block = jnp.concatenate([keys, values], axis=1)
            block = jnp.where(crow == LIVE_CH, high, jnp.where(crow == LIVE_CH + 1, line - high, block))
            part[g * NX + j] = block.astype(BF16)
    terms = [remote(part.at[(tp + e) % 8], rsbuf.at[8 - e], tp_peers[e - 1]) for e in range(1, 8)]

    pick = iota((CH, T), 1) == iota((CH, T), 0) * NX + x
    cos_k, sin_k = tables(pos_ref, inv_ref, pick)

    via_plus.wait_recv()
    partner_top = remote(via.at[0], feat.at[1, 0, top], y_plus)
    via_minus.wait_recv()
    partner_low = remote(via.at[1], feat.at[1, 0, low], y_minus)

    summed = part[tp].astype(F32)
    for e in range(1, 8):
        terms[e - 1].wait_recv()
        summed = summed + rsbuf[8 - e].astype(F32)
    line = summed[LIVE_CH : LIVE_CH + 1] + summed[LIVE_CH + 1 : LIVE_CH + 2]
    squares = jnp.sum(jnp.where(crow == clane, line, 0.0), axis=1, keepdims=True)
    scaled = summed * lax.rsqrt(squares / D + 1e-06)
    live = (iota((CH, HW), 0) * NX + x < total) & (iota((CH, HW), 0) < LIVE_CH)
    keys = rope(scaled[:, :HW], cos_k, sin_k)
    keys = jnp.where(live, keys, keys[0:1])
    values = jnp.where(live, scaled[:, HW:], 0.0)
    kv_out[0, 0, 0] = jnp.concatenate([keys, values], axis=1).astype(BF16)

    y_moves = [remote(kv_out.at[0, 0, 0], kv_out.at[0, 0, NY - e], y_peers[e - 1]) for e in range(1, NY)]
    ups, downs = {}, {}

    def send_up(t, dy):
        ups[t, dy] = remote(kv_out.at[-t % NZ, 0, dy], kv_out.at[(-t - 1) % NZ, 0, dy], up)

    def send_down(t, dy):
        downs[t, dy] = remote(kv_out.at[t, 0, dy], kv_out.at[t + 1, 0, dy], down)

    send_up(0, 0)
    send_down(0, 0)

    def pass_on(g):
        from_left[g].wait_recv()
        a = remote(feat.at[g, 3, top], feat.at[g, 2, top], right)
        from_right[g].wait_recv()
        b = remote(feat.at[g, 1, low], feat.at[g, 2, low], left)
        return a, b

    far = [pass_on(0), None]
    partner_top.wait_recv()
    partner_low.wait_recv()
    from_left[1] = remote(feat.at[1, 0], feat.at[1, 3], right)
    from_right[1] = remote(feat.at[1, 0], feat.at[1, 1], left)
    for e in range(1, NY):
        y_moves[e - 1].wait_recv()
        send_up(0, NY - e)
        send_down(0, NY - e)
    siblings = [remote(kv_out.at[0, 0], kv_out.at[0, 1], sibling)]

    fetch.wait()
    pick = iota((T, T), 1) == iota((T, T), 0)
    cos_q, sin_q = tables(pos_ref, inv_ref, pick)
    acc = [jnp.zeros((T, 2 * HW), F32), jnp.zeros((T, 1), F32)]

    def add(g, d):
        piece = ((h + g) % 2) * NX + (x + d) % NX
        wide = feat[g, d].astype(F32)
        acc[1] = acc[1] + jnp.sum(wide * wide, axis=1, keepdims=True)
        gained = (wide * gain_ref[pl.ds(piece, 1)]).astype(BF16)
        acc[0] = acc[0] + jnp.dot(gained, qw[pl.ds(pl.multiple_of(piece * DS, DS), DS)], preferred_element_type=F32)

    def z_step(t):
        for dy in range(NY):
            ups[t - 1, dy].wait_recv()
            if t < 3 or dy < 2:
                send_up(t, dy)
            downs[t - 1, dy].wait_recv()
            if t < 3 or dy >= 2:
                send_down(t, dy)
        siblings.append(remote(kv_out.at[NZ - t, 0], kv_out.at[NZ - t, 1], sibling))
        siblings.append(remote(kv_out.at[t, 0], kv_out.at[t, 1], sibling))

    add(0, 0)
    z_step(1)
    add(0, 3)
    add(0, 1)
    far[0][0].wait_recv()
    far[0][1].wait_recv()
    far[1] = pass_on(1)
    add(0, 2)
    add(1, 0)
    z_step(2)
    add(1, 3)
    add(1, 1)
    z_step(3)
    far[1][0].wait_recv()
    far[1][1].wait_recv()
    add(1, 2)
    queries = acc[0] * (lax.rsqrt(acc[1] / D + 1e-06) * QSCALE)
    q_out[0] = jnp.concatenate(
        [rope(queries[:, :HW], cos_q, sin_q), rope(queries[:, HW:], cos_q, sin_q)], axis=1
    ).astype(BF16)
    q_moves = [
        remote(q_out.at[0], q_out.at[NX - e], device(at, x=(x + e) % NX)) for e in range(1, NX)
    ]
    for dy in range(NY):
        (ups if dy < 2 else downs)[3, dy].wait_recv()
    siblings.append(remote(kv_out.at[4, 0], kv_out.at[4, 1], sibling))
    for copy in siblings + q_moves:
        copy.wait_recv()
    for copy in copies:
        copy.wait_send()


COPIES = 2 + 2 + 2 + 2 + 4 + 2 + 7 + 3 + 28 + 8 + 3


def attend_kernel(
    vcount, acount, q_ref, kv_ref, o_ref, stat_ref, kc, vc, vown, m_ref, acc_ref
):
    at = place()
    ctx, x = at["ctx"], at["x"]

    def live_rows(s):
        return (vcount[s] + acount[s] - x + NX - 1) // NX

    crow = iota((CH, HW), 0)

    def compact(j, off):
        dz, dc, dy = j // (NC * NY), (j // NY) % NC, j % NY
        s = (((at["yl"] + dy) % NY) * NZ + (at["z"] + dz) % NZ) * NC + (at["core"] + dc) % NC
        rows = live_rows(s)
        block = kv_ref[dz, dc, dy]
        where = pl.ds(pl.multiple_of(off, 16), CH)
        kc[where] = block[:, :HW]
        vc[where, :HW] = block[:, HW:]
        vc[where, HW:] = jnp.where(crow < rows, 1.0, 0.0).astype(BF16)
        return off + jnp.where(s < ctx, ((rows + 15) // 16) * 16, 0)

    count = lax.fori_loop(0, NZ * NC * NY, compact, jnp.int32(0))
    tail = pl.ds(pl.multiple_of(count, 16), KB)
    kc[tail] = jnp.broadcast_to(kc[0:1], (KB, HW))
    vc[tail] = jnp.zeros((KB, 2 * HW), BF16)

    own = kv_ref[0, 0, 0]
    own_rows = live_rows(ctx)
    vown[:, :HW] = own[:, HW:]
    vown[:, HW:] = jnp.where(crow < own_rows, 1.0, 0.0).astype(BF16)
    key = iota((T, CH), 1)
    counted = (key * NX + x <= iota((T, CH), 0)) & (key < own_rows)
    nt = (((1,), (1,)), ((), ()))
    blocks = [(j, k) for j in range(NX) for k in range(2)]
    for b, (j, k) in enumerate(blocks):
        q = q_ref[j, :, k * HW : (k + 1) * HW]
        s = lax.dot_general(q, own[:, :HW], nt, preferred_element_type=F32)
        s = jnp.where(counted, s, NEG)
        m = jnp.max(s, axis=1, keepdims=True)
        p = jnp.where(counted, jnp.exp2(s - m), 0.0).astype(BF16)
        m_ref[b] = m
        acc_ref[b] = jnp.dot(p, vown[...], preferred_element_type=F32)

    def step(i, carry):
        rows = pl.ds(pl.multiple_of(i * KB, KB), KB)
        for b, (j, k) in enumerate(blocks):
            q = q_ref[j, :, k * HW : (k + 1) * HW]
            s = lax.dot_general(q, kc[rows], nt, preferred_element_type=F32)
            before = m_ref[b]
            m = jnp.maximum(before, jnp.max(s, axis=1, keepdims=True))
            p = jnp.exp2(s - m).astype(BF16)
            m_ref[b] = m
            acc_ref[b] = acc_ref[b] * jnp.exp2(before - m) + jnp.dot(p, vc[rows], preferred_element_type=F32)
        return carry

    lax.fori_loop(0, (count + KB - 1) // KB, step, 0)

    eye = iota((T, T), 0) == iota((T, T), 1)
    stat_ref[...] = jnp.zeros_like(stat_ref)
    for b, (j, k) in enumerate(blocks):
        acc = acc_ref[b]
        total = acc[:, HW : HW + 1]
        some = total > 0.0
        safe = jnp.where(some, total, 1.0)
        o_ref[j, :, k * HW : (k + 1) * HW] = (acc[:, :HW] / safe).astype(BF16)
        level = jnp.where(some, m_ref[b] + jnp.log2(safe), NEG)
        stat_ref[j, k : k + 1, :T] = jnp.sum(jnp.where(eye, level, 0.0), axis=0, keepdims=True)


def combine_kernel(vcount, acount, o_ref, stat_ref, out_ref, obuf, sbuf, ssem, rsem):
    at = place()
    ctx, x = at["ctx"], at["x"]
    peers = [device(at, x=(x + e) % NX) for e in range(1, NX)]
    barrier = pltpu.get_barrier_semaphore()
    for other in peers:
        pl.semaphore_signal(barrier, inc=1, device_id=other, device_id_type=MESH)
    pl.semaphore_wait(barrier, len(peers))
    copies = []
    for e in range(1, NX):
        for n, (src, dst) in enumerate([(o_ref, obuf), (stat_ref, sbuf)]):
            copy = pltpu.make_async_remote_copy(
                src_ref=src.at[e], dst_ref=dst.at[NX - e], send_sem=ssem.at[n, e], recv_sem=rsem.at[n, e],
                device_id=peers[e - 1], device_id_type=MESH,
            )
            copy.start()
            copies.append(copy)
    eye = iota((T, T), 0) == iota((T, T), 1)

    def column(line):
        return jnp.sum(jnp.where(eye, line[:, :T], 0.0), axis=1, keepdims=True)

    for copy in copies:
        copy.wait_recv()
    live = iota((T, HW), 0) < vcount[ctx] + acount[ctx]
    for k in range(2):
        cols = slice(k * HW, (k + 1) * HW)
        levels = [column((stat_ref if j == 0 else sbuf)[j, k : k + 1]) for j in range(NX)]
        peak = functools.reduce(jnp.maximum, levels)
        shares = [jnp.exp2(level - peak) for level in levels]
        parts = [(o_ref if j == 0 else obuf)[j, :, cols].astype(F32) for j in range(NX)]
        summed = sum(s * a for s, a in zip(shares, parts))
        out_ref[0, :, cols] = jnp.where(live, summed / sum(shares), 0.0).astype(BF16)
    for copy in copies:
        copy.wait_send()


def whole():
    return pl.BlockSpec(memory_space=pltpu.VMEM)


def scalars():
    return pl.BlockSpec(memory_space=pltpu.SMEM)


LIMIT = 48 * 1024 * 1024


def per_device(
    vision_rows, audio_rows, vision_count, audio_count, position_ids, audio_proj, norm_gain, q_weight, key_value_weight
):
    lane = np.arange(HW) % (HW // 2)
    inverse = np.exp(-math.log(1000000.0) * 2.0 * lane / HW).astype(np.float32)[None]
    q_all, kv_all = pl.pallas_call(
        gather_kernel,
        out_shape=(
            jax.ShapeDtypeStruct((NX, T, 2 * HW), BF16),
            jax.ShapeDtypeStruct((NZ, NC, NY, CH, 2 * HW), BF16),
        ),
        in_specs=[scalars(), scalars()] + [whole()] * 7 + [pl.BlockSpec(memory_space=pl.ANY)],
        out_specs=(whole(), whole()),
        scratch_shapes=[
            pltpu.VMEM((T, DS), BF16),
            pltpu.VMEM((2, NX, T, DS), BF16),
            pltpu.VMEM((2, HALF, DS), BF16),
            pltpu.VMEM((8, CH, 2 * HW), BF16),
            pltpu.VMEM((8, CH, 2 * HW), BF16),
            pltpu.VMEM((D, 2 * HW), BF16),
            pltpu.SemaphoreType.DMA,
            pltpu.SemaphoreType.DMA((COPIES,)),
            pltpu.SemaphoreType.DMA((COPIES,)),
        ],
        compiler_params=pltpu.CompilerParams(collective_id=0, has_side_effects=True, vmem_limit_bytes=LIMIT),
        name="gather",
    )(
        vision_count, audio_count, position_ids, jnp.asarray(inverse), norm_gain.reshape(8, DS),
        vision_rows, audio_rows, audio_proj, key_value_weight, q_weight,
    )
    longest = NZ * NC * NY * CH + KB
    o_part, stats = pl.pallas_call(
        attend_kernel,
        out_shape=(
            jax.ShapeDtypeStruct((NX, T, 2 * HW), BF16),
            jax.ShapeDtypeStruct((NX, 8, 256), F32),
        ),
        in_specs=[scalars(), scalars(), whole(), whole()],
        out_specs=(whole(), whole()),
        scratch_shapes=[
            pltpu.VMEM((longest, HW), BF16),
            pltpu.VMEM((longest, 2 * HW), BF16),
            pltpu.VMEM((CH, 2 * HW), BF16),
            pltpu.VMEM((8, T, 1), F32),
            pltpu.VMEM((8, T, 2 * HW), F32),
        ],
        compiler_params=pltpu.CompilerParams(vmem_limit_bytes=LIMIT),
        name="attend",
    )(vision_count, audio_count, q_all, kv_all)
    return pl.pallas_call(
        combine_kernel,
        out_shape=jax.ShapeDtypeStruct((1, T, 2 * HW), BF16),
        in_specs=[scalars(), scalars(), whole(), whole()],
        out_specs=whole(),
        scratch_shapes=[
            pltpu.VMEM((NX, T, 2 * HW), BF16),
            pltpu.VMEM((NX, 8, 256), F32),
            pltpu.SemaphoreType.DMA((2, NX)),
            pltpu.SemaphoreType.DMA((2, NX)),
        ],
        compiler_params=pltpu.CompilerParams(collective_id=1, has_side_effects=True, vmem_limit_bytes=LIMIT),
        name="combine",
    )(vision_count, audio_count, o_part, stats)


def solution(mesh):
    placed = (
        P("ctx", None, "tp"),
        P("ctx", None, None),
        P(),
        P(),
        P(None, "ctx", None),
        P(None, "tp"),
        P(),
        P(None, "tp"),
        P("tp", None),
    )
    return jax.shard_map(
        per_device, mesh=mesh, in_specs=placed, out_specs=P("ctx", None, "tp"), check_vma=False
    )
```

time: 791 us -> 87.7 us (0.11); the launches traced: 782 us -> 87.4 us
  waiting for transfers between devices: 413 us -> 0 us
  other arithmetic: 193 us -> 0 us
  matrix products: 152 us -> 0 us
  Pallas kernels: 0 us -> 81.5 us
  between operations: 13.4 us -> 0.14 us
    all_gather x4 -> x0, waiting for transfers between devices: 412 us -> none  [the longest x1 120 us: attend(): value_piece = lax.all_gather(value_part, 'ctx', axis=0, tiled=True)]
    dot_general x131 -> x0, matrix products: 152 us -> none  [the longest x64 72.8 us: update(): jnp.einsum('hqk,kd->hqd', weights.astype(jnp.bfloat16), value_block, pref...]
    pallas_call x0 -> x3, Pallas kernels: none -> 81.5 us  [the longest x1 56.9 us: per_device(): pl.pallas_call(gather_kernel, out_shape=(jax.ShapeDtypeStruct((NX, T, 2 *...]
    add x192 -> x0, other arithmetic: 78.8 us -> none  [the longest x64 41.4 us: update(): key_pos = stretch_start + row_offset + local_rows]
    reduce_sum x131 -> x0, other arithmetic: 57.8 us -> none  [the longest x66 48 us: lookup(): return jnp.sum(jnp.where(stretch_ids == wanted, table, 0))]
    lt x65 -> x0, other arithmetic: 44.9 us -> none  [the longest x64 44.3 us: update(): key_live = row_offset + local_rows < stretch_total]
    and x64 -> x0, other arithmetic: 8.12 us -> none  [update(): counted = (key_pos[None, :] <= query_pos[:, None]) & key_live[None, :]]
  transfers between devices with their start and end apart: 4 -> 0, of which waited for: 4 -> 0; matrix products, arithmetic and copies ran while one was open for 1% -> 0% of each run, Pallas kernels for 0% -> 0%
where the time goes in v1:
time: 87.7 us; the launch traced here: 87.4 us
  Pallas kernels  81.5 us (93%)
  local copies, waits for them, and re-layouts  5.79 us (7%)
    pallas_call x1, Pallas kernels, per_device(): pl.pallas_call(gather_kernel, out_shape=(jax.ShapeDtypeStruct((NX, T, 2 *...  56.9 us
    pallas_call x1, Pallas kernels, per_device(): pl.pallas_call(attend_kernel, out_shape=(jax.ShapeDtypeStruct((NX, T, 2 *...  15 us
    pallas_call x1, Pallas kernels, per_device(): pl.pallas_call(combine_kernel, out_shape=jax.ShapeDtypeStruct((1, T, 2 *...  9.6 us
    unnamed x20, local copies, waits for them, and re-layouts  4.85 us

profile of v1, /device:TPU:56, one launch (start us, length us, event | category | flops | bytes accessed | tf_op | source)
XLA Modules:
  0.0 87.4 jit_solution(5358793821594889669)
XLA Ops:
  0.0 0.0 copy-start.8
  0.0 0.0 copy-start.6
  0.0 0.0 copy-start.5
  0.0 0.0 copy-start.1
  0.0 0.0 copy-start.7
  0.0 0.0 copy-start.4
  0.0 0.0 copy-start.3
  0.0 0.9 %reshape.3.gain_ref = f32[8,448]{1,0:T(8,128)S(1)} reshape(f32[3584]{0:T(1024)} %param.16) | data formatting | bytes 28672 | tf_op jit(solution)/shard_map/reshape | solution.py:402
  1.0 1.6 %copy.11.proj_ref = bf16[1280,448]{1,0:T(8,128)(2,1)S(1)} copy(bf16[1280,448]{0,1:T(8,128)(2,1)} %param.15) | data formatting | bytes 2293760 | tf_op args[5]
  2.6 0.0 copy-done.8
  2.6 0.0 copy-done.6
  2.6 0.0 copy-done.5
  2.6 0.0 copy-done.1
  2.6 0.0 copy-done.7
  2.6 0.0 copy-done.4
  2.6 0.0 copy-done.3
  2.6 0.0 copy-start.2
  2.7 1.0 %copy-done.2 = bf16[448,512]{1,0:T(8,128)(2,1)S(1)} copy-done((bf16[448,512]{1,0:T(8,128)(2,1)S(1)}, bf16[448,512]{1,0:T(8,128)(2,1)}, u32[]{:S(2)}) %copy-start.2) | copy-done | bytes 458776
  3.7 56.9 %gather.1 = (bf16[4,224,256]{2,1,0:T(8,128)(2,1)S(1)}, bf16[8,2,4,64,256]{4,3,2,1,0:T(8,128)(2,1)}) custom-call(s32[64]{0:T(128)S(1)} %copy-done.5, s32[64]{0:T(128)S(1)} %copy-done.6, s32[3,1,224]{2,1,0:T(1,128)S(1)} %copy-done.7, f32[1,128]{1,0:T(1,128)S(1)} %copy-done.8, f32[8,448]{1,0:T(8,128)S(1)} %reshape.3.gain_ref, ...), custom_call_target="tpu_custom_call" | custom-call | tf_op jit(solution)/shard_map/gather/pallas_call | solution.py:380
  60.5 0.0 copy-start
  60.5 1.6 %copy-done = bf16[8,2,4,64,256]{4,3,2,1,0:T(8,128)(2,1)S(1)} copy-done((bf16[8,2,4,64,256]{4,3,2,1,0:T(8,128)(2,1)S(1)}, bf16[8,2,4,64,256]{4,3,2,1,0:T(8,128)(2,1)}, u32[]{:S(2)}) %copy-start) | copy-done | bytes 2097176
  62.1 15.0 %attend.1 = (bf16[4,224,256]{2,1,0:T(8,128)(2,1)S(1)}, f32[4,8,256]{2,1,0:T(8,128)S(1)}) custom-call(s32[64]{0:T(128)S(1)} %copy-done.5, s32[64]{0:T(128)S(1)} %copy-done.6, bf16[4,224,256]{2,1,0:T(8,128)(2,1)S(1)} %get-tuple-element.9.q_ref, bf16[8,2,4,64,256]{4,3,2,1,0:T(8,128)(2,1)S(1)} %copy-done), custom_call_target="tpu_custom_call" | custom-call | tf_op jit(solution)/shard_map/attend/pallas_call | solution.py:406
  77.2 9.6 %combine.1 = bf16[1,224,256]{2,1,0:T(8,128)(2,1)S(1)} custom-call(s32[64]{0:T(128)S(1)} %copy-done.5, s32[64]{0:T(128)S(1)} %copy-done.6, bf16[4,224,256]{2,1,0:T(8,128)(2,1)S(1)} %get-tuple-element.11.o_ref, f32[4,8,256]{2,1,0:T(8,128)S(1)} %get-tuple-element.12.stat_ref), custom_call_target="tpu_custom_call" | custom-call | tf_op jit(solution)/shard_map/combine/pallas_call | solution.py:424
  86.8 0.6 copy.13
Async XLA Ops:
  0.0 2.6 %copy-start.8 = (f32[1,128]{1,0:T(1,128)S(1)}, f32[1,128]{1,0:T(1,128)}, u32[]{:S(2)}) copy-start(f32[1,128]{1,0:T(1,128)} %constant.2.clone.inv_ref) | copy-start | bytes 1540
  0.0 2.6 %copy-start.6 = (s32[64]{0:T(128)S(1)}, s32[64]{0:T(128)}, u32[]{:S(2)}) copy-start(s32[64]{0:T(128)} %acount.5) | copy-start | bytes 772
  0.0 2.6 %copy-start.5 = (s32[64]{0:T(128)S(1)}, s32[64]{0:T(128)}, u32[]{:S(2)}) copy-start(s32[64]{0:T(128)} %vcount.5) | copy-start | bytes 772
  0.0 2.6 %copy-start.1 = (bf16[3584,256]{1,0:T(8,128)(2,1)S(1)}, bf16[3584,256]{1,0:T(8,128)(2,1)}, u32[]{:S(2)}) copy-start(bf16[3584,256]{1,0:T(8,128)(2,1)} %qw_hbm.1) | copy-start | bytes 5505028
  0.0 2.6 %copy-start.7 = (s32[3,1,224]{2,1,0:T(1,128)S(1)}, s32[3,1,224]{2,1,0:T(1,128)}, u32[]{:S(2)}) copy-start(s32[3,1,224]{2,1,0:T(1,128)} %pos_ref.1) | copy-start | bytes 8068
  0.0 2.6 %copy-start.4 = (bf16[1,64,1280]{2,1,0:T(8,128)(2,1)S(1)}, bf16[1,64,1280]{2,1,0:T(8,128)(2,1)}, u32[]{:S(2)}) copy-start(bf16[1,64,1280]{2,1,0:T(8,128)(2,1)} %audio_ref.1) | copy-start | bytes 491524
  0.0 2.6 %copy-start.3 = (bf16[1,160,448]{2,1,0:T(8,128)(2,1)S(1)}, bf16[1,160,448]{2,1,0:T(8,128)(2,1)}, u32[]{:S(2)}) copy-start(bf16[1,160,448]{2,1,0:T(8,128)(2,1)} %vision_ref.1) | copy-start | bytes 430084
  2.6 1.0 %copy-start.2 = (bf16[448,512]{1,0:T(8,128)(2,1)S(1)}, bf16[448,512]{1,0:T(8,128)(2,1)}, u32[]{:S(2)}) copy-start(bf16[448,512]{1,0:T(8,128)(2,1)} %kvw_ref.1) | copy-start | bytes 1376260
  60.5 1.6 %copy-start = (bf16[8,2,4,64,256]{4,3,2,1,0:T(8,128)(2,1)S(1)}, bf16[8,2,4,64,256]{4,3,2,1,0:T(8,128)(2,1)}, u32[]{:S(2)}) copy-start(bf16[8,2,4,64,256]{4,3,2,1,0:T(8,128)(2,1)} %get-tuple-element.10.kv_ref) | copy-start | bytes 6291460

commit v2 on v0

v2 whole, which is shorter than its diff:
```python
import functools
import math

import jax
import jax.numpy as jnp
import numpy as np
from jax import lax
from jax.experimental import pallas as pl
from jax.experimental.pallas import tpu as pltpu
from jax.sharding import PartitionSpec as P

HW = 128
MESH = pl.DeviceIdType.MESH
F32 = jnp.float32
BF16 = jnp.bfloat16

NY, NZ, NC, NX = 4, 8, 2, 4
VC, AC, T = 160, 64, 224
AW = 1280
DS, D = 448, 3584
CH = 64
LIVE_CH = T // NX
TOP, LOW = pl.ds(0, T // 2), pl.ds(T // 2, T // 2)
PIECES = [pl.ds(0, 64), pl.ds(64, 48), pl.ds(112, 64), pl.ds(176, 48)]
NT = (((1,), (1,)), ((), ()))
MASKED, LEAST = -1e30, -1e29
QSCALE = HW**-0.5 * math.log2(math.e)


def iota(shape, dim):
    return lax.broadcasted_iota(jnp.int32, shape, dim)


def place():
    ctx, tp = lax.axis_index("ctx"), lax.axis_index("tp")
    return dict(yl=ctx // (NZ * NC), z=(ctx // NC) % NZ, core=ctx % NC, h=tp // NX, x=tp % NX, ctx=ctx, tp=tp)


def device(at, yl=None, z=None, core=None, h=None, x=None):
    yl = at["yl"] if yl is None else yl
    z = at["z"] if z is None else z
    core = at["core"] if core is None else core
    h = at["h"] if h is None else h
    x = at["x"] if x is None else x
    return ((yl * NZ + z) * NC + core, h * NX + x)


def swap_halves(a):
    return jnp.concatenate([a[:, HW // 2 :], a[:, : HW // 2]], axis=1)


def rope(a, cos, sin):
    return a * cos + swap_halves(a) * sin


def tables(pos_ref, inv_ref, pick):
    rows = pick.shape[0]
    ids = [
        jnp.sum(jnp.where(pick, pos_ref[k].astype(F32), 0.0), axis=1, keepdims=True) for k in range(3)
    ]
    lane = iota((rows, HW), 1)
    freq = lane % (HW // 2)
    first = HW // 8
    second = (HW // 2 - first) // 2
    chosen = jnp.where(freq < first, ids[0], jnp.where(freq < first + second, ids[1], ids[2]))
    angle = chosen * inv_ref[...]
    sin = jnp.sin(angle)
    return jnp.cos(angle), jnp.where(lane < HW // 2, -sin, sin)


def gain_rows(gain_ref):
    g = gain_ref[...]
    half = HW // 2
    rows = []
    for u in range(4):
        r = [g[7 * u + k : 7 * u + k + 1] for k in range(7)]
        rows.append(jnp.concatenate([r[0], r[1], r[2], r[3][:, :half]], axis=1))
        rows.append(jnp.concatenate([r[3][:, half:], r[4], r[5], r[6]], axis=1))
    return jnp.concatenate(rows, axis=0)


def layer_kernel(
    vcount, acount, pos_hbm, inv_ref, gain_ref, vision_hbm, audio_hbm, proj_hbm, kvw_hbm, qw_hbm,
    out_ref,
    pos_ref, vision_ref, audio_ref, proj_ref, kvw_ref, qw,
    stacked, gains, feat, part, xbuf, ysend, ybuf, q_all, kv, bias, m_ref, acc_ref, o_part, stat, obuf, sbuf,
    fetch_sem, ssem, rsem,
):
    at = place()
    ctx, tp, x, h = at["ctx"], at["tp"], at["x"], at["h"]
    fetches = []
    for src, dst in [
        (audio_hbm, audio_ref), (proj_hbm, proj_ref), (vision_hbm, vision_ref), (kvw_hbm, kvw_ref), (pos_hbm, pos_ref), (qw_hbm, qw)
    ]:
        fetches.append(pltpu.make_async_copy(src, dst, fetch_sem.at[len(fetches)]))
        fetches[-1].start()

    right = device(at, x=(x + 1) % NX)
    left = device(at, x=(x + 3) % NX)
    up = device(at, z=(at["z"] + 1) % NZ)
    down = device(at, z=(at["z"] + 7) % NZ)
    sibling = device(at, core=1 - at["core"])
    partner = device(at, h=1 - h)
    x_peers = [device(at, x=(x + e) % NX) for e in range(1, NX)]
    y_peers = [device(at, yl=(at["yl"] + e) % NY) for e in range(1, NY)]
    greeted = [up, down, sibling, partner] + x_peers + y_peers
    barrier = pltpu.get_barrier_semaphore()
    for other in greeted:
        pl.semaphore_signal(barrier, inc=1, device_id=other, device_id_type=MESH)

    copies = []

    def remote(src, dst, to):
        i = len(copies)
        copy = pltpu.make_async_remote_copy(
            src_ref=src, dst_ref=dst, send_sem=ssem.at[i], recv_sem=rsem.at[i], device_id=to, device_id_type=MESH
        )
        copies.append(copy)
        copy.start()
        return copy

    vision_here = vcount[ctx]
    total = vision_here + acount[ctx]
    fetches[0].wait()
    fetches[1].wait()
    stacked[VC:] = lax.dot_general(audio_ref[0], proj_ref[...], NT, preferred_element_type=F32).astype(BF16)
    fetches[2].wait()
    stacked[:VC] = vision_ref[0]

    def picked(slot, valid):
        source = jnp.where(slot < vision_here, slot, VC + slot - vision_here)
        hit = (iota((slot.shape[0], T), 1) == source) & (slot < total) & valid
        onehot = jnp.where(hit, 1.0, 0.0).astype(BF16)
        return jnp.dot(onehot, stacked[...], preferred_element_type=F32)

    slot = iota((T, 1), 0)
    feat[0, 0] = picked(slot, slot >= 0).astype(BF16)
    pl.semaphore_wait(barrier, len(greeted))
    crossed = {p: remote(feat.at[0, 0, PIECES[p]], feat.at[1, 0, PIECES[p]], partner) for p in (0, 2, 1, 3)}

    row = iota((NX * CH, 1), 0)
    chunk_row = row % CH
    chunked = picked(chunk_row * NX + row // CH, chunk_row < LIVE_CH)
    squares = jnp.sum(chunked * chunked, axis=1, keepdims=True)
    gains[...] = gain_rows(gain_ref)
    gained = (chunked * gains[pl.ds(tp, 1)]).astype(BF16)
    fetches[3].wait()
    term = jnp.dot(gained, kvw_ref[...], preferred_element_type=F32)
    crow, clane = iota((CH, 4 * HW), 0), iota((CH, 4 * HW), 1)
    for j in range(NX):
        rows = slice(j * CH, (j + 1) * CH)
        line = jnp.sum(jnp.where(crow == clane % (2 * HW), squares[rows], 0.0), axis=0, keepdims=True)
        high = line.astype(BF16).astype(F32)
        t = term[rows]
        block = jnp.concatenate(
            [t[:, :HW], t[:, 2 * HW : 3 * HW], t[:, HW : 2 * HW], t[:, 3 * HW :]], axis=1
        )
        block = jnp.where(crow == LIVE_CH, high, jnp.where(crow == LIVE_CH + 1, line - high, block))
        part[j] = block.astype(BF16)
    terms = [remote(part.at[(x + e) % NX], xbuf.at[NX - e], x_peers[e - 1]) for e in (2, 1, 3)]
    from_left = [[remote(feat.at[0, 0], feat.at[0, 3], right)]]
    from_right = [[remote(feat.at[0, 0], feat.at[0, 1], left)]]

    fetches[4].wait()
    pick = iota((CH, T), 1) == iota((CH, T), 0) * NX + x
    cos_k, sin_k = tables(pos_ref, inv_ref, pick)

    dz, lane = iota((NZ, NC * NY * CH), 0), iota((NZ, NC * NY * CH), 1)
    dc, dy, i = lane // (NY * CH), (lane // CH) % NY, lane % CH
    stretch = (((at["yl"] + dy) % NY) * NZ + (at["z"] + dz) % NZ) * NC + (at["core"] + dc) % NC
    lengths = jnp.zeros_like(stretch)
    for k in range(NY * NZ * NC):
        lengths = jnp.where(stretch == k, vcount[k] + acount[k], lengths)
    counted = (stretch < ctx) & (i < LIVE_CH) & (i * NX + x < lengths)
    bias[...] = jnp.where(counted, 0.0, MASKED)

    summed = part[x].astype(F32)
    for copy, e in zip(terms, (2, 1, 3)):
        copy.wait_recv()
        summed = summed + xbuf[NX - e].astype(F32)
    first, second = summed[:, : 2 * HW], summed[:, 2 * HW :]
    mine = jnp.where(h == 0, first, second)
    other = jnp.where(h == 0, second, first)
    drow, dlane = iota((CH, 2 * HW), 0), iota((CH, 2 * HW), 1)

    def square_line(a):
        return a[LIVE_CH : LIVE_CH + 1] + a[LIVE_CH + 1 : LIVE_CH + 2]

    line = square_line(other)
    high = line.astype(BF16).astype(F32)
    ysend[...] = jnp.where(drow == LIVE_CH, high, jnp.where(drow == LIVE_CH + 1, line - high, other)).astype(BF16)
    across = remote(ysend, ybuf, partner)

    for copy in from_left[0] + from_right[0]:
        copy.wait_recv()
    far = [
        remote(feat.at[0, 3, TOP], feat.at[0, 2, TOP], right),
        remote(feat.at[0, 1, LOW], feat.at[0, 2, LOW], left),
    ]
    from_left.append({})
    from_right.append({})
    for p in (0, 2, 1, 3):
        crossed[p].wait_recv()
        from_left[1][p] = remote(feat.at[1, 0, PIECES[p]], feat.at[1, 3, PIECES[p]], right)
        from_right[1][p] = remote(feat.at[1, 0, PIECES[p]], feat.at[1, 1, PIECES[p]], left)

    across.wait_recv()
    summed = mine + ybuf[...].astype(F32)
    line = square_line(summed)
    squares = jnp.sum(jnp.where(drow == dlane, line, 0.0), axis=1, keepdims=True)
    scaled = summed * lax.rsqrt(squares / D + 1e-06)
    filled = iota((CH, HW), 0) < LIVE_CH
    keys = jnp.where(filled, rope(scaled[:, :HW], cos_k, sin_k), 0.0)
    values = jnp.where(filled, scaled[:, HW:], 0.0)
    kv[0, 0, 0] = jnp.concatenate([keys, values], axis=1).astype(BF16)

    y_moves = [remote(kv.at[0, 0, 0], kv.at[0, 0, NY - e], y_peers[e - 1]) for e in range(1, NY)]
    ups, downs = {}, {}

    def send_up(t, first, size):
        where = pl.ds(first, size)
        ups[t, first] = remote(kv.at[-t % NZ, 0, where], kv.at[(-t - 1) % NZ, 0, where], up)

    def send_down(t, first, size):
        where = pl.ds(first, size)
        downs[t, first] = remote(kv.at[t, 0, where], kv.at[t + 1, 0, where], down)

    send_up(0, 0, 1)
    send_down(0, 0, 1)

    fetches[5].wait()
    pick = iota((T, T), 1) == iota((T, T), 0)
    cos_q, sin_q = tables(pos_ref, inv_ref, pick)
    sums = [jnp.zeros((T, 2 * HW), F32), jnp.zeros((T, 1), F32)]

    def add(g, d):
        piece = ((h + g) % 2) * NX + (x + d) % NX
        wide = feat[g, d].astype(F32)
        sums[1] = sums[1] + jnp.sum(wide * wide, axis=1, keepdims=True)
        gained = (wide * gains[pl.ds(piece, 1)]).astype(BF16)
        sums[0] = sums[0] + jnp.dot(gained, qw[pl.ds(pl.multiple_of(piece * DS, DS), DS)], preferred_element_type=F32)

    add(0, 0)
    for e in (3, 1, 2):
        y_moves[e - 1].wait_recv()
        send_up(0, NY - e, 1)
        send_down(0, NY - e, 1)
    siblings = {0: remote(kv.at[0, 0], kv.at[0, 1], sibling)}

    def to_sibling(d):
        siblings[d] = remote(kv.at[d, 0], kv.at[d, 1], sibling)

    def z_step(t):
        for first in (0, 2):
            came = [0, 1] if first == 0 else [2, 3]
            for d in came if t == 1 else [first]:
                ups[t - 1, d].wait_recv()
            if t < 3 or first == 0:
                send_up(t, first, 2)
            for d in came if t == 1 else [first]:
                downs[t - 1, d].wait_recv()
            if t < 3 or first == 2:
                send_down(t, first, 2)
        to_sibling(NZ - t)
        to_sibling(t)

    add(1, 0)
    for p in (0, 1):
        from_left[1][p].wait_recv()
        far.append(remote(feat.at[1, 3, PIECES[p]], feat.at[1, 2, PIECES[p]], right))
        from_right[1][p + 2].wait_recv()
        far.append(remote(feat.at[1, 1, PIECES[p + 2]], feat.at[1, 2, PIECES[p + 2]], left))
    z_step(1)
    add(0, 3)
    add(0, 1)
    far[0].wait_recv()
    far[1].wait_recv()
    add(0, 2)
    for p in (2, 3):
        from_left[1][p].wait_recv()
        from_right[1][p - 2].wait_recv()
    add(1, 3)
    add(1, 1)
    z_step(2)
    for copy in far[2:]:
        copy.wait_recv()
    add(1, 2)
    queries = sums[0] * (lax.rsqrt(sums[1] / D + 1e-06) * QSCALE)
    for k in range(2):
        q_all[0, k] = rope(queries[:, k * HW : (k + 1) * HW], cos_q, sin_q).astype(BF16)
    q_moves = {NX - e: remote(q_all.at[0], q_all.at[NX - e], x_peers[e - 1]) for e in (1, 3, 2)}

    key = iota((T, CH), 1)
    own_counted = (key * NX + x <= iota((T, CH), 0)) & (key < LIVE_CH) & (key * NX + x < total)

    def with_ones(values):
        return jnp.concatenate([values, jnp.ones(values.shape, BF16)], axis=1)

    def begin(j):
        own = kv[0, 0, 0]
        for k in range(2):
            s = lax.dot_general(q_all[j, k], own[:, :HW], NT, preferred_element_type=F32)
            s = jnp.where(own_counted, s, MASKED)
            m = jnp.maximum(jnp.max(s, axis=1, keepdims=True), LEAST)
            m_ref[j, k] = m
            acc_ref[j, k] = jnp.dot(jnp.exp2(s - m).astype(BF16), with_ones(own[:, HW:]), preferred_element_type=F32)

    def attend(j, start, count):
        def one(n, carry):
            pair = (start + n) % (NZ // 2)
            block = jnp.concatenate([kv[pair * 2 + u].reshape(NC * NY * CH, 2 * HW) for u in range(2)], axis=0)
            keys, values = block[:, :HW], with_ones(block[:, HW:])
            mask = jnp.concatenate([bias[pl.ds(pair * 2, 1)], bias[pl.ds(pair * 2 + 1, 1)]], axis=1)
            scores = [lax.dot_general(q_all[j, k], keys, NT, preferred_element_type=F32) + mask for k in range(2)]
            for k in range(2):
                before = m_ref[j, k]
                m = jnp.maximum(before, jnp.max(scores[k], axis=1, keepdims=True))
                p = jnp.exp2(scores[k] - m).astype(BF16)
                m_ref[j, k] = m
                acc_ref[j, k] = acc_ref[j, k] * jnp.exp2(before - m) + jnp.dot(p, values, preferred_element_type=F32)
            return carry

        lax.fori_loop(0, count, one, 0)

    eye = iota((T, T), 0) == iota((T, T), 1)
    stat[...] = jnp.zeros_like(stat)

    def finish(j):
        for k in range(2):
            acc = acc_ref[j, k]
            weight = acc[:, HW : HW + 1]
            some = weight > 0.0
            safe = jnp.where(some, weight, 1.0)
            o_part[j, k] = (acc[:, :HW] / safe).astype(BF16)
            level = jnp.where(some, m_ref[j, k] + jnp.log2(safe), MASKED)
            stat[j, k, 0:1, :T] = jnp.sum(jnp.where(eye, level, 0.0), axis=0, keepdims=True)

    begin(0)
    z_step(3)
    for d in (0, 1, 7, 6):
        siblings[d].wait_recv()
    attend(0, 3, 2)
    for n, j in enumerate((1, 3, 2)):
        q_moves[j].wait_recv()
        begin(j)
        attend(j, 3, 2)
        if n == 0:
            ups[3, 0].wait_recv()
            downs[3, 2].wait_recv()
            to_sibling(4)
    for d in (2, 3, 5, 4):
        siblings[d].wait_recv()
    parts = {}
    for j in (2, 1, 3):
        attend(j, 1, 2)
        finish(j)
        parts[NX - j] = [
            remote(stat.at[j], sbuf.at[NX - j], x_peers[j - 1]), remote(o_part.at[j], obuf.at[NX - j], x_peers[j - 1])
        ]
    attend(0, 1, 2)
    finish(0)

    def column(line):
        return jnp.sum(jnp.where(eye, line[:, :T], 0.0), axis=1, keepdims=True)

    for j in (2, 3, 1):
        for copy in parts[j]:
            copy.wait_recv()
    live = iota((T, HW), 0) < total
    for k in range(2):
        levels = [stat[0, k][0:1]] + [sbuf[j, k][0:1] for j in range(1, NX)]
        peak = functools.reduce(jnp.maximum, levels)
        shares = [jnp.exp2(level - peak) for level in levels]
        whole_share = sum(shares)
        pieces = [o_part[0, k]] + [obuf[j, k] for j in range(1, NX)]
        summed = sum(column(s / whole_share) * a.astype(F32) for s, a in zip(shares, pieces))
        out_ref[0, :, k * HW : (k + 1) * HW] = jnp.where(live, summed, 0.0).astype(BF16)
    for copy in copies:
        copy.wait_send()


COPIES = 4 + 3 + 2 + 1 + 2 + 8 + 3 + 18 + 8 + 4 + 3 + 6


def whole():
    return pl.BlockSpec(memory_space=pltpu.VMEM)


def anywhere():
    return pl.BlockSpec(memory_space=pl.ANY)


def scalars():
    return pl.BlockSpec(memory_space=pltpu.SMEM)


LIMIT = 54 * 1024 * 1024


def per_device(
    vision_rows, audio_rows, vision_count, audio_count, position_ids, audio_proj, norm_gain, q_weight, key_value_weight
):
    lane = np.arange(HW) % (HW // 2)
    inverse = np.exp(-math.log(1000000.0) * 2.0 * lane / HW).astype(np.float32)[None]
    return pl.pallas_call(
        layer_kernel,
        out_shape=jax.ShapeDtypeStruct((1, T, 2 * HW), BF16),
        in_specs=[scalars(), scalars(), anywhere(), whole(), whole()] + [anywhere()] * 5,
        out_specs=whole(),
        scratch_shapes=[
            pltpu.VMEM((3, 1, T), jnp.int32),
            pltpu.VMEM((1, VC, DS), BF16),
            pltpu.VMEM((1, AC, AW), BF16),
            pltpu.VMEM((DS, AW), BF16),
            pltpu.VMEM((DS, 4 * HW), BF16),
            pltpu.VMEM((D, 2 * HW), BF16),
            pltpu.VMEM((T, DS), BF16),
            pltpu.VMEM((8, DS), F32),
            pltpu.VMEM((2, NX, T, DS), BF16),
            pltpu.VMEM((NX, CH, 4 * HW), BF16),
            pltpu.VMEM((NX, CH, 4 * HW), BF16),
            pltpu.VMEM((CH, 2 * HW), BF16),
            pltpu.VMEM((CH, 2 * HW), BF16),
            pltpu.VMEM((NX, 2, T, HW), BF16),
            pltpu.VMEM((NZ, NC, NY, CH, 2 * HW), BF16),
            pltpu.VMEM((NZ, NC * NY * CH), F32),
            pltpu.VMEM((NX, 2, T, 1), F32),
            pltpu.VMEM((NX, 2, T, 2 * HW), F32),
            pltpu.VMEM((NX, 2, T, HW), BF16),
            pltpu.VMEM((NX, 2, 8, 2 * HW), F32),
            pltpu.VMEM((NX, 2, T, HW), BF16),
            pltpu.VMEM((NX, 2, 8, 2 * HW), F32),
            pltpu.SemaphoreType.DMA((6,)),
            pltpu.SemaphoreType.DMA((COPIES,)),
            pltpu.SemaphoreType.DMA((COPIES,)),
        ],
        compiler_params=pltpu.CompilerParams(collective_id=0, has_side_effects=True, vmem_limit_bytes=LIMIT),
        name="layer",
    )(
        vision_count, audio_count, position_ids, jnp.asarray(inverse), norm_gain.reshape(D // HW, HW),
        vision_rows, audio_rows, audio_proj.T, key_value_weight, q_weight,
    )


def solution(mesh):
    placed = (
        P("ctx", None, "tp"),
        P("ctx", None, None),
        P(),
        P(),
        P(None, "ctx", None),
        P(None, "tp"),
        P(),
        P(None, "tp"),
        P("tp", None),
    )
    return jax.shard_map(
        per_device, mesh=mesh, in_specs=placed, out_specs=P("ctx", None, "tp"), check_vma=False
    )
```

time: 791 us -> 69.1 us (0.09); the launches traced: 782 us -> 68.6 us
  waiting for transfers between devices: 413 us -> 0 us
  other arithmetic: 193 us -> 0 us
  matrix products: 152 us -> 0 us
  Pallas kernels: 0 us -> 67.1 us
  between operations: 13.4 us -> 0.01 us
    all_gather x4 -> x0, waiting for transfers between devices: 412 us -> none  [the longest x1 120 us: attend(): value_piece = lax.all_gather(value_part, 'ctx', axis=0, tiled=True)]
    dot_general x131 -> x0, matrix products: 152 us -> none  [the longest x64 72.8 us: update(): jnp.einsum('hqk,kd->hqd', weights.astype(jnp.bfloat16), value_block, pref...]
    add x192 -> x0, other arithmetic: 78.8 us -> none  [the longest x64 41.4 us: update(): key_pos = stretch_start + row_offset + local_rows]
    pallas_call x0 -> x1, Pallas kernels: none -> 67.1 us  [per_device(): pl.pallas_call(layer_kernel, out_shape=jax.ShapeDtypeStruct((1, T, 2 * HW...]
    reduce_sum x131 -> x0, other arithmetic: 57.8 us -> none  [the longest x66 48 us: lookup(): return jnp.sum(jnp.where(stretch_ids == wanted, table, 0))]
    lt x65 -> x0, other arithmetic: 44.9 us -> none  [the longest x64 44.3 us: update(): key_live = row_offset + local_rows < stretch_total]
    and x64 -> x0, other arithmetic: 8.12 us -> none  [update(): counted = (key_pos[None, :] <= query_pos[:, None]) & key_live[None, :]]
  transfers between devices with their start and end apart: 4 -> 0, of which waited for: 4 -> 0; matrix products, arithmetic and copies ran while one was open for 1% -> 0% of each run, Pallas kernels for 0% -> 0%
where the time goes in v2:
time: 69.1 us; the launch traced here: 68.6 us
  Pallas kernels  67.1 us (97%)
  local copies, waits for them, and re-layouts  1.55 us (2%)
    pallas_call x1, Pallas kernels, per_device(): pl.pallas_call(layer_kernel, out_shape=jax.ShapeDtypeStruct((1, T, 2 * HW...  67.1 us
    unnamed x1, local copies, waits for them, and re-layouts  1.55 us

profile of v2, /device:TPU:56, one launch (start us, length us, event | category | flops | bytes accessed | tf_op | source)
XLA Modules:
  0.0 68.6 jit_solution(16456641559205762853)
XLA Ops:
  0.0 67.1 %layer.1 = bf16[1,224,256]{2,1,0:T(8,128)(2,1)} custom-call(s32[64]{0:T(128)} %vcount.1, s32[64]{0:T(128)} %acount.1, s32[3,1,224]{2,1,0:T(1,128)} %pos_hbm.1, f32[1,128]{1,0:T(1,128)} %constant.2.clone.inv_ref, f32[28,128]{1,0:T(8,128)} %bitcast.3, bf16[1,160,448]{2,1,0:T(8,128)(2,1)} %vision_hbm.1, bf16[1,64,1280]{2,1,0:T(8,128)(2,1)} %audio_hbm.1, ...), custom_call_target="tpu_custom_call" | custom-call | tf_op jit(solution)/shard_map/layer/pallas_call | solution.py:405
  67.1 1.6 %copy.12 = bf16[1,224,256]{2,1,0:T(8,128)(2,1)} copy(bf16[1,224,256]{2,1,0:T(8,128)(2,1)} %layer.1) | data formatting | bytes 229376

commit v3 on v2

--- a/solution.py
+++ b/solution.py
@@ -135,8 +135,6 @@
 
     slot = iota((T, 1), 0)
     feat[0, 0] = picked(slot, slot >= 0).astype(BF16)
-    pl.semaphore_wait(barrier, len(greeted))
-    crossed = {p: remote(feat.at[0, 0, PIECES[p]], feat.at[1, 0, PIECES[p]], partner) for p in (0, 2, 1, 3)}
 
     row = iota((NX * CH, 1), 0)
     chunk_row = row % CH
@@ -146,20 +144,28 @@
     gained = (chunked * gains[pl.ds(tp, 1)]).astype(BF16)
     fetches[3].wait()
     term = jnp.dot(gained, kvw_ref[...], preferred_element_type=F32)
-    crow, clane = iota((CH, 4 * HW), 0), iota((CH, 4 * HW), 1)
+    drow, dlane = iota((CH, 2 * HW), 0), iota((CH, 2 * HW), 1)
     for j in range(NX):
         rows = slice(j * CH, (j + 1) * CH)
-        line = jnp.sum(jnp.where(crow == clane % (2 * HW), squares[rows], 0.0), axis=0, keepdims=True)
+        line = jnp.sum(jnp.where(drow == dlane, squares[rows], 0.0), axis=0, keepdims=True)
         high = line.astype(BF16).astype(F32)
-        t = term[rows]
-        block = jnp.concatenate(
-            [t[:, :HW], t[:, 2 * HW : 3 * HW], t[:, HW : 2 * HW], t[:, 3 * HW :]], axis=1
-        )
-        block = jnp.where(crow == LIVE_CH, high, jnp.where(crow == LIVE_CH + 1, line - high, block))
-        part[j] = block.astype(BF16)
-    terms = [remote(part.at[(x + e) % NX], xbuf.at[NX - e], x_peers[e - 1]) for e in (2, 1, 3)]
-    from_left = [[remote(feat.at[0, 0], feat.at[0, 3], right)]]
-    from_right = [[remote(feat.at[0, 0], feat.at[0, 1], left)]]
+        for g in range(2):
+            block = jnp.concatenate(
+                [term[rows, g * HW : (g + 1) * HW], term[rows, (2 + g) * HW : (3 + g) * HW]], axis=1
+            )
+            block = jnp.where(drow == LIVE_CH, high, jnp.where(drow == LIVE_CH + 1, line - high, block))
+            part[j, g] = block.astype(BF16)
+    pl.semaphore_wait(barrier, len(greeted))
+
+    def send_terms(own):
+        half = h if own else 1 - h
+        return [remote(part.at[(x + e) % NX, half], xbuf.at[own, NX - e], x_peers[e - 1]) for e in (2, 1, 3)]
+
+    terms = [send_terms(0)]
+    crossed = {p: remote(feat.at[0, 0, PIECES[p]], feat.at[1, 0, PIECES[p]], partner) for p in range(4)}
+    terms.append(send_terms(1))
+    from_left = remote(feat.at[0, 0], feat.at[0, 3], right)
+    from_right = remote(feat.at[0, 0], feat.at[0, 1], left)
 
     fetches[4].wait()
     pick = iota((CH, T), 1) == iota((CH, T), 0) * NX + x
@@ -174,35 +180,67 @@
     counted = (stretch < ctx) & (i < LIVE_CH) & (i * NX + x < lengths)
     bias[...] = jnp.where(counted, 0.0, MASKED)
 
-    summed = part[x].astype(F32)
-    for copy, e in zip(terms, (2, 1, 3)):
-        copy.wait_recv()
-        summed = summed + xbuf[NX - e].astype(F32)
-    first, second = summed[:, : 2 * HW], summed[:, 2 * HW :]
-    mine = jnp.where(h == 0, first, second)
-    other = jnp.where(h == 0, second, first)
-    drow, dlane = iota((CH, 2 * HW), 0), iota((CH, 2 * HW), 1)
+    fetches[5].wait()
+    pick = iota((T, T), 1) == iota((T, T), 0)
+    cos_q, sin_q = tables(pos_ref, inv_ref, pick)
+    sums, weights = {}, {}
+
+    def add(half, g, d):
+        rows = pl.ds(half * (T // 2), T // 2)
+        piece = ((h + g) % 2) * NX + (x + d) % NX
+        wide = feat[g, d, rows].astype(F32)
+        square = jnp.sum(wide * wide, axis=1, keepdims=True)
+        gained = (wide * gains[pl.ds(piece, 1)]).astype(BF16)
+        term = jnp.dot(gained, qw[pl.ds(pl.multiple_of(piece * DS, DS), DS)], preferred_element_type=F32)
+        sums[half] = sums[half] + term if half in sums else term
+        weights[half] = weights[half] + square if half in weights else square
+
+    q_moves = {}
+
+    def send_queries(half):
+        rows = slice(half * (T // 2), (half + 1) * (T // 2))
+        where = pl.ds(half * (T // 2), T // 2)
+        queries = sums[half] * (lax.rsqrt(weights[half] / D + 1e-06) * QSCALE)
+        for k in range(2):
+            q_all[0, k, where] = rope(queries[:, k * HW : (k + 1) * HW], cos_q[rows], sin_q[rows]).astype(BF16)
+        for e in (2, 1, 3):
+            q_moves[half, NX - e] = remote(q_all.at[0, :, where], q_all.at[NX - e, :, where], x_peers[e - 1])
+
+    add(0, 0, 0)
+    add(1, 0, 0)
+    def add_terms(own):
+        total_term = part[x, h if own else 1 - h].astype(F32)
+        for copy, e in zip(terms[own], (2, 1, 3)):
+            copy.wait_recv()
+            total_term = total_term + xbuf[own, NX - e].astype(F32)
+        return total_term
 
     def square_line(a):
         return a[LIVE_CH : LIVE_CH + 1] + a[LIVE_CH + 1 : LIVE_CH + 2]
 
+    other = add_terms(0)
     line = square_line(other)
     high = line.astype(BF16).astype(F32)
     ysend[...] = jnp.where(drow == LIVE_CH, high, jnp.where(drow == LIVE_CH + 1, line - high, other)).astype(BF16)
     across = remote(ysend, ybuf, partner)
-
-    for copy in from_left[0] + from_right[0]:
-        copy.wait_recv()
+    mine = add_terms(1)
+
+    from_left.wait_recv()
+    from_right.wait_recv()
     far = [
         remote(feat.at[0, 3, TOP], feat.at[0, 2, TOP], right),
         remote(feat.at[0, 1, LOW], feat.at[0, 2, LOW], left),
     ]
-    from_left.append({})
-    from_right.append({})
-    for p in (0, 2, 1, 3):
+    spread = {}
+    for p in range(4):
         crossed[p].wait_recv()
-        from_left[1][p] = remote(feat.at[1, 0, PIECES[p]], feat.at[1, 3, PIECES[p]], right)
-        from_right[1][p] = remote(feat.at[1, 0, PIECES[p]], feat.at[1, 1, PIECES[p]], left)
+        for e in (2, 1, 3):
+            spread[p, NX - e] = remote(feat.at[1, 0, PIECES[p]], feat.at[1, NX - e, PIECES[p]], x_peers[e - 1])
+
+    def land(half, d):
+        spread[2 * half, d].wait_recv()
+        spread[2 * half + 1, d].wait_recv()
+        add(half, 1, d)
 
     across.wait_recv()
     summed = mine + ybuf[...].astype(F32)
@@ -228,19 +266,11 @@
     send_up(0, 0, 1)
     send_down(0, 0, 1)
 
-    fetches[5].wait()
-    pick = iota((T, T), 1) == iota((T, T), 0)
-    cos_q, sin_q = tables(pos_ref, inv_ref, pick)
-    sums = [jnp.zeros((T, 2 * HW), F32), jnp.zeros((T, 1), F32)]
-
-    def add(g, d):
-        piece = ((h + g) % 2) * NX + (x + d) % NX
-        wide = feat[g, d].astype(F32)
-        sums[1] = sums[1] + jnp.sum(wide * wide, axis=1, keepdims=True)
-        gained = (wide * gains[pl.ds(piece, 1)]).astype(BF16)
-        sums[0] = sums[0] + jnp.dot(gained, qw[pl.ds(pl.multiple_of(piece * DS, DS), DS)], preferred_element_type=F32)
-
-    add(0, 0)
+    for half in range(2):
+        add(half, 0, 3)
+        add(half, 0, 1)
+        far[half].wait_recv()
+        add(half, 0, 2)
     for e in (3, 1, 2):
         y_moves[e - 1].wait_recv()
         send_up(0, NY - e, 1)
@@ -264,31 +294,16 @@
         to_sibling(NZ - t)
         to_sibling(t)
 
-    add(1, 0)
-    for p in (0, 1):
-        from_left[1][p].wait_recv()
-        far.append(remote(feat.at[1, 3, PIECES[p]], feat.at[1, 2, PIECES[p]], right))
-        from_right[1][p + 2].wait_recv()
-        far.append(remote(feat.at[1, 1, PIECES[p + 2]], feat.at[1, 2, PIECES[p + 2]], left))
+    add(0, 1, 0)
+    add(1, 1, 0)
+    for d in (1, 3, 2):
+        land(0, d)
+    send_queries(0)
     z_step(1)
-    add(0, 3)
-    add(0, 1)
-    far[0].wait_recv()
-    far[1].wait_recv()
-    add(0, 2)
-    for p in (2, 3):
-        from_left[1][p].wait_recv()
-        from_right[1][p - 2].wait_recv()
-    add(1, 3)
-    add(1, 1)
+    for d in (1, 3, 2):
+        land(1, d)
+    send_queries(1)
     z_step(2)
-    for copy in far[2:]:
-        copy.wait_recv()
-    add(1, 2)
-    queries = sums[0] * (lax.rsqrt(sums[1] / D + 1e-06) * QSCALE)
-    for k in range(2):
-        q_all[0, k] = rope(queries[:, k * HW : (k + 1) * HW], cos_q, sin_q).astype(BF16)
-    q_moves = {NX - e: remote(q_all.at[0], q_all.at[NX - e], x_peers[e - 1]) for e in (1, 3, 2)}
 
     key = iota((T, CH), 1)
     own_counted = (key * NX + x <= iota((T, CH), 0)) & (key < LIVE_CH) & (key * NX + x < total)
@@ -305,22 +320,32 @@
             m_ref[j, k] = m
             acc_ref[j, k] = jnp.dot(jnp.exp2(s - m).astype(BF16), with_ones(own[:, HW:]), preferred_element_type=F32)
 
-    def attend(j, start, count):
+    def attend(blocks, start, count, width=1):
         def one(n, carry):
-            pair = (start + n) % (NZ // 2)
-            block = jnp.concatenate([kv[pair * 2 + u].reshape(NC * NY * CH, 2 * HW) for u in range(2)], axis=0)
+            block = jnp.concatenate([kv[d].reshape(NC * NY * CH, 2 * HW) for d in blocks], axis=0)
             keys, values = block[:, :HW], with_ones(block[:, HW:])
-            mask = jnp.concatenate([bias[pl.ds(pair * 2, 1)], bias[pl.ds(pair * 2 + 1, 1)]], axis=1)
-            scores = [lax.dot_general(q_all[j, k], keys, NT, preferred_element_type=F32) + mask for k in range(2)]
-            for k in range(2):
+            mask = jnp.concatenate([bias[d : d + 1] for d in blocks], axis=1)
+            heads = [(start + n * width + u, k) for u in range(width) for k in range(2)]
+
+            def score(j, k):
+                return lax.dot_general(q_all[j, k], keys, NT, preferred_element_type=F32) + mask
+
+            ahead = [score(*heads[0]), score(*heads[1])]
+            for i, (j, k) in enumerate(heads):
+                scores = ahead.pop(0)
+                if i + 2 < len(heads):
+                    ahead.append(score(*heads[i + 2]))
                 before = m_ref[j, k]
-                m = jnp.maximum(before, jnp.max(scores[k], axis=1, keepdims=True))
-                p = jnp.exp2(scores[k] - m).astype(BF16)
+                m = jnp.maximum(before, jnp.max(scores, axis=1, keepdims=True))
+                p = jnp.exp2(scores - m).astype(BF16)
                 m_ref[j, k] = m
                 acc_ref[j, k] = acc_ref[j, k] * jnp.exp2(before - m) + jnp.dot(p, values, preferred_element_type=F32)
             return carry
 
-        lax.fori_loop(0, count, one, 0)
+        if count == width:
+            one(0, 0)
+        else:
+            lax.fori_loop(0, count // width, one, 0)
 
     eye = iota((T, T), 0) == iota((T, T), 1)
     stat[...] = jnp.zeros_like(stat)
@@ -333,31 +358,36 @@
             safe = jnp.where(some, weight, 1.0)
             o_part[j, k] = (acc[:, :HW] / safe).astype(BF16)
             level = jnp.where(some, m_ref[j, k] + jnp.log2(safe), MASKED)
-            stat[j, k, 0:1, :T] = jnp.sum(jnp.where(eye, level, 0.0), axis=0, keepdims=True)
+            stat[j, k : k + 1, :T] = jnp.sum(jnp.where(eye, level, 0.0), axis=0, keepdims=True)
 
     begin(0)
+    siblings[0].wait_recv()
+    siblings[1].wait_recv()
+    attend((0, 1), 0, 1)
+    for j in (1, 3, 2):
+        q_moves[0, j].wait_recv()
+        q_moves[1, j].wait_recv()
+        begin(j)
+    attend((0, 1), 1, 3, 3)
     z_step(3)
-    for d in (0, 1, 7, 6):
+    siblings[7].wait_recv()
+    siblings[6].wait_recv()
+    attend((7, 6), 0, 4, 4)
+    ups[3, 0].wait_recv()
+    downs[3, 2].wait_recv()
+    to_sibling(4)
+    for d in (2, 3, 5):
         siblings[d].wait_recv()
-    attend(0, 3, 2)
-    for n, j in enumerate((1, 3, 2)):
-        q_moves[j].wait_recv()
-        begin(j)
-        attend(j, 3, 2)
-        if n == 0:
-            ups[3, 0].wait_recv()
-            downs[3, 2].wait_recv()
-            to_sibling(4)
-    for d in (2, 3, 5, 4):
-        siblings[d].wait_recv()
+    attend((2, 3, 5), 1, 3, 3)
+    siblings[4].wait_recv()
     parts = {}
     for j in (2, 1, 3):
-        attend(j, 1, 2)
+        attend((4,), j, 1)
         finish(j)
         parts[NX - j] = [
             remote(stat.at[j], sbuf.at[NX - j], x_peers[j - 1]), remote(o_part.at[j], obuf.at[NX - j], x_peers[j - 1])
         ]
-    attend(0, 1, 2)
+    attend((2, 3, 5, 4), 0, 1)
     finish(0)
 
     def column(line):
@@ -368,7 +398,7 @@
             copy.wait_recv()
     live = iota((T, HW), 0) < total
     for k in range(2):
-        levels = [stat[0, k][0:1]] + [sbuf[j, k][0:1] for j in range(1, NX)]
+        levels = [stat[0, k : k + 1]] + [sbuf[j, k : k + 1] for j in range(1, NX)]
         peak = functools.reduce(jnp.maximum, levels)
         shares = [jnp.exp2(level - peak) for level in levels]
         whole_share = sum(shares)
@@ -379,7 +409,7 @@
         copy.wait_send()
 
 
-COPIES = 4 + 3 + 2 + 1 + 2 + 8 + 3 + 18 + 8 + 4 + 3 + 6
+COPIES = 4 + 6 + 2 + 1 + 2 + 12 + 3 + 18 + 8 + 6 + 6
 
 
 def whole():
@@ -417,8 +447,8 @@
             pltpu.VMEM((T, DS), BF16),
             pltpu.VMEM((8, DS), F32),
             pltpu.VMEM((2, NX, T, DS), BF16),
-            pltpu.VMEM((NX, CH, 4 * HW), BF16),
-            pltpu.VMEM((NX, CH, 4 * HW), BF16),
+            pltpu.VMEM((NX, 2, CH, 2 * HW), BF16),
+            pltpu.VMEM((2, NX, CH, 2 * HW), BF16),
             pltpu.VMEM((CH, 2 * HW), BF16),
             pltpu.VMEM((CH, 2 * HW), BF16),
             pltpu.VMEM((NX, 2, T, HW), BF16),
@@ -427,9 +457,9 @@
             pltpu.VMEM((NX, 2, T, 1), F32),
             pltpu.VMEM((NX, 2, T, 2 * HW), F32),
             pltpu.VMEM((NX, 2, T, HW), BF16),
-            pltpu.VMEM((NX, 2, 8, 2 * HW), F32),
+            pltpu.VMEM((NX, 8, 2 * HW), F32),
             pltpu.VMEM((NX, 2, T, HW), BF16),
-            pltpu.VMEM((NX, 2, 8, 2 * HW), F32),
+            pltpu.VMEM((NX, 8, 2 * HW), F32),
             pltpu.SemaphoreType.DMA((6,)),
             pltpu.SemaphoreType.DMA((COPIES,)),
             pltpu.SemaphoreType.DMA((COPIES,)),

time: 69.1 us -> 67.3 us (0.974)
  the two profiles are of different devices: /device:TPU:56 before, /device:TPU:2 now
where the time goes in v3:
time: 67.3 us; the launch traced here: 67.1 us
  Pallas kernels  65.5 us (97%)
  local copies, waits for them, and re-layouts  1.55 us (2%)
    pallas_call x1, Pallas kernels, per_device(): pl.pallas_call(layer_kernel, out_shape=jax.ShapeDtypeStruct((1, T, 2 * HW...  65.5 us
    unnamed x1, local copies, waits for them, and re-layouts  1.55 us

profile of v3, /device:TPU:2, one launch (start us, length us, event | category | flops | bytes accessed | tf_op | source)
XLA Modules:
  0.0 67.1 jit_solution(7753156459368211981)
XLA Ops:
  0.0 65.5 %layer.1 = bf16[1,224,256]{2,1,0:T(8,128)(2,1)} custom-call(s32[64]{0:T(128)} %vcount.1, s32[64]{0:T(128)} %acount.1, s32[3,1,224]{2,1,0:T(1,128)} %pos_hbm.1, f32[1,128]{1,0:T(1,128)} %constant.2.clone.inv_ref, f32[28,128]{1,0:T(8,128)} %bitcast.3, bf16[1,160,448]{2,1,0:T(8,128)(2,1)} %vision_hbm.1, bf16[1,64,1280]{2,1,0:T(8,128)(2,1)} %audio_hbm.1, ...), custom_call_target="tpu_custom_call" | custom-call | tf_op jit(solution)/shard_map/layer/pallas_call | solution.py:435
  65.6 1.6 %copy.12 = bf16[1,224,256]{2,1,0:T(8,128)(2,1)} copy(bf16[1,224,256]{2,1,0:T(8,128)(2,1)} %layer.1) | data formatting | bytes 229376
